TPU v7x, 512 devices: a whole 4x4x16 slice. The times are simulated.
512 devices in a mesh: tile: 32 (over y, x, core), member: 16 (over z).
Axes of the slice: x: 4, y: 4, z: 16, core: 2. Of those that a mesh axis runs over, the one named last changes fastest.
Arguments:
- hx: bfloat16 [512, 131072], P('member', 'tile'), may hold values from -6 to 6
- obs_value: bfloat16 [131072], P('tile'), may hold values from -8 to 8
- obs_rinv: bfloat16 [131072], P('tile'), may hold values from 0.29882812 to 4
- obs_index: int32 [512, 1024], P('tile'), may hold values from 128 to 6015, as said below
- loc_weight: float32 [512, 1024], P(('tile', 'member')), may hold values from 0.05 to 1
- state: bfloat16 [512, 524288], P('member', 'tile'), may hold values from -6 to 6
Outputs:
- analysis: bfloat16 [512, 524288], P('member', 'tile')
Inputs may be any that keep to these rules, and one draw needn't show every extreme that they name: `obs_index`: row p lists 1024 distinct positions in the pool of tile p // 16: positions 0 .. 1023 are the last 1024 observations of the tile before it, the next 4096 the tile's own, the last 1024 the first observations of the tile after it; the tiles form a closed band. All positions of a row lie within 2048 consecutive positions.
All inputs are finite; a program needn't handle non-finite values.
Results may differ from a plain program's by a relative error of at most 0.012.
The roundings to bfloat16 on the way count: a program that leaves them out, or rounds other values in their place, can miss the bound.
Values may be sent and summed in bfloat16 or wider, within the bound.
A program may use at most 64 MiB of HBM per device.

v0:
```python
import jax
import jax.numpy as jnp
from jax import lax
from jax.sharding import PartitionSpec as P

LOC = 1024
NS_ITERS = 3


def with_halo(block, sides, width):
    for axis, dim in sides:
        count = lax.axis_size(axis)
        forward = [(i, i + 1) for i in range(count - 1)]
        forward.append((count - 1, 0))
        backward = [(target, source) for source, target in forward]
        low = lax.ppermute(
            lax.slice_in_dim(block, block.shape[dim] - width, None, axis=dim), axis, forward
        )
        high = lax.ppermute(lax.slice_in_dim(block, 0, width, axis=dim), axis, backward)
        block = jnp.concatenate([low, block, high], axis=dim)
    return block


def product_f32(left, right, dims):
    return lax.dot_general(
        left.astype(jnp.float32),
        right.astype(jnp.float32),
        (dims, ((), ())),
        precision=lax.Precision.HIGHEST,
        preferred_element_type=jnp.float32,
    )


def analysis(obs_block, obs_pair, loc_row):
    members = obs_block.shape[0]
    block_f = obs_block.astype(jnp.float32)
    obs_mean = jnp.mean(block_f, axis=0)
    obs_root = jnp.sqrt(obs_pair[1].astype(jnp.float32) * loc_row)
    scaled = ((block_f - obs_mean) * obs_root).astype(jnp.bfloat16)
    innovation = (obs_pair[0].astype(jnp.float32) - obs_mean) * obs_root
    gram_matrix = product_f32(scaled, scaled, ((1,), (1,)))
    identity = jnp.eye(members, dtype=jnp.float32)
    system = gram_matrix + (members - 1.0) * identity
    projection = jnp.dot(scaled.astype(jnp.float32), innovation, precision=lax.Precision.HIGHEST)
    norm_a = jnp.sqrt(jnp.sum(system * system))
    upper_iter = system / norm_a
    lower_iter = identity
    for sweep in range(NS_ITERS):
        upper_b = upper_iter.astype(jnp.bfloat16)
        lower_b = lower_iter.astype(jnp.bfloat16)
        product = product_f32(lower_b, upper_b, ((1,), (0,)))
        half_step = (1.5 * identity - 0.5 * product).astype(jnp.bfloat16)
        if sweep + 1 < NS_ITERS:
            upper_iter = product_f32(upper_b, half_step, ((1,), (0,)))
        lower_iter = product_f32(half_step, lower_b, ((1,), (0,)))
    invroot = lower_iter / jnp.sqrt(norm_a)
    inner_w = jnp.dot(invroot, projection, precision=lax.Precision.HIGHEST)
    mean_w = jnp.dot(invroot, inner_w, precision=lax.Precision.HIGHEST)
    transform = jnp.sqrt(members - 1.0) * invroot + mean_w[:, None]
    return transform.astype(jnp.bfloat16)


def transform_state(transform, state_block):
    block_f = state_block.astype(jnp.float32)
    state_mean = jnp.mean(block_f, axis=0)
    state_pert = (block_f - state_mean).astype(jnp.bfloat16)
    combined = product_f32(transform, state_pert, ((0,), (0,)))
    return (state_mean + combined).astype(jnp.bfloat16)


def on_device(hx, obs_value, obs_rinv, obs_index, loc_weight, state):
    ens_dev = hx.shape[0]
    member_pos = lax.axis_index("member")
    stacked = jnp.concatenate([hx, obs_value[None, :], obs_rinv[None, :]], axis=0)
    obs_pool = with_halo(stacked, (("tile", 1),), LOC)
    own_index = lax.dynamic_index_in_dim(obs_index, member_pos, 0, keepdims=False)
    obs_pair = jnp.take(obs_pool[ens_dev:], own_index, axis=1)
    all_rows = lax.all_gather(obs_pool[:ens_dev], "member", axis=0, tiled=True)
    obs_block = jnp.take(all_rows, own_index, axis=1)
    transform = analysis(obs_block, obs_pair, loc_weight[0])
    group_count = obs_index.shape[0]
    state_split = state.reshape(ens_dev, group_count, state.shape[1] // group_count)
    updated = transform_state(
        transform,
        lax.all_to_all(state_split, "member", split_axis=1, concat_axis=0, tiled=True)[:, 0, :],
    )
    result = lax.all_to_all(updated[:, None, :], "member", split_axis=0, concat_axis=1, tiled=True)
    return result.reshape(ens_dev, state.shape[1])


def solution(mesh):
    in_specs = (
        P("member", "tile"),
        P("tile"),
        P("tile"),
        P("tile", None),
        P(("tile", "member"), None),
        P("member", "tile"),
    )
    out_specs = P("member", "tile")
    return jax.shard_map(
        on_device, mesh=mesh, in_specs=in_specs, out_specs=out_specs, check_vma=False
    )
```

profile of v0, /device:TPU:24, one launch (start us, length us, event | category | flops | bytes accessed | tf_op | source)
XLA Modules:
  0.0 249.0 jit_solution(11522932096585671620)
XLA Ops:
  8.1 0.9 pad_maximum_fusion.3
  9.0 1.9 collective-permute-start
  10.9 5.8 %collective-permute-start.1 = (bf16[34,1024]{1,0:T(8,128)(2,1)S(1)}, bf16[34,1024]{1,0:T(8,128)(2,1)S(1)}, u32[]{:S(2)}, u32[]{:S(2)}) collective-permute-start(bf16[34,1024]{1,0:T(8,128)(2,1)S(1)} %get-tuple-element.8), channel_id=1, source_target_pairs={{16,0},{32,16},{48,32},{64,48},{80,64},{96,80},{112,96},{128,112},... | collective-permute-start | bytes 208904 | tf_op jit(solution)/shard_map/ppermute | solution.py:19
  16.8 1.9 collective-permute-done.1
  18.7 1.0 pad_maximum_fusion
  19.7 0.8 slice.28
  20.5 1.1 copy.44
  21.6 15.2 %all-to-all-start = ((bf16[32,16,1024]{2,0,1:T(8,128)(2,1)}), bf16[32,16,1024]{2,0,1:T(8,128)(2,1)S(1)}, u32[]{:S(2)}, u32[]{:S(2)}) async-start(bf16[32,16,1024]{2,0,1:T(8,128)(2,1)} %bitcast.59), calls=%async_computation | async-start | bytes 2097152 | tf_op jit(solution)/shard_map/all_to_all | solution.py:85
  37.7 0.9 copy.34
  38.6 3.2 %gather_fusion.1 = bf16[1024,2]{1,0:T(8,128)(2,1)S(1)} fusion(bf16[2,6144]{0,1:T(8,128)(2,1)S(1)} %copy.34, s32[1024]{0:T(1024)S(1)} %broadcast_clamp_fusion), kind=kCustom, calls=%fused_computation.1 | custom fusion | bytes 12288 | tf_op jit(solution)/shard_map/jit(_take)/gather | solution.py:77
  42.9 53.0 %all-to-all-done = bf16[32,16,1024]{2,0,1:T(8,128)(2,1)S(1)} async-done(((bf16[32,16,1024]{2,0,1:T(8,128)(2,1)}), bf16[32,16,1024]{2,0,1:T(8,128)(2,1)S(1)}, u32[]{:S(2)}, u32[]{:S(2)}) %all-to-all-start) | async-done | bytes 1048608 | tf_op jit(solution)/shard_map/all_to_all | solution.py:85
  96.4 54.4 %all-gather.2.cloned.1.call-done = bf16[512,6144]{1,0:T(8,128)(2,1)} async-done(((bf16[32,6144]{1,0:T(8,128)(2,1)}), bf16[512,6144]{1,0:T(8,128)(2,1)}) %all-gather.2.cloned.1.call-update) | async-done | bytes 6291472 | tf_op jit(solution)/shard_map/all_gather | solution.py:78
  150.8 8.6 %copy.33 = bf16[512,6144]{0,1:T(8,128)(2,1)} copy(bf16[512,6144]{1,0:T(8,128)(2,1)} %all-gather.2.cloned.1.call-done) | data formatting | bytes 12582912 | tf_op jit(solution)/shard_map/all_gather | solution.py:78
  159.4 7.6 %gather_fusion = bf16[1024,512]{1,0:T(8,128)(2,1)S(1)} fusion(bf16[512,6144]{0,1:T(8,128)(2,1)} %copy.33, s32[1024]{0:T(1024)S(1)} %broadcast_clamp_fusion), kind=kCustom, calls=%fused_computation | custom fusion | bytes 2101248 | tf_op jit(solution)/shard_map/jit(_take)/gather | solution.py:79
  167.5 0.9 fusion.1
  168.4 1.5 multiply_reduce_fusion
  174.7 1.0 convolution_bitcast_fusion
  175.7 1.0 fusion.11
  176.7 0.8 fusion.3
  178.1 1.4 reduce.8
  179.5 0.8 reshape.88
  180.3 59.4 %all_to_all.24 = bf16[16,2,16384]{2,1,0:T(2,128)(2,1)S(1)} all-to-all(bf16[16,2,16384]{2,1,0:T(2,128)(2,1)S(1)} %reshape.88), channel_id=1, replica_groups=mesh['tile'=32,'member'=16] {'member'}, dimensions={0} | all-to-all | bytes 2097152 | tf_op jit(solution)/shard_map/all_to_all | solution.py:87
  239.7 1.0 reshape.89
  241.1 1.1 copy.41
  (38 shorter events, 9.5 us)
Async XLA Ops:
  6.5 14.0 %copy-start.1 = (bf16[32,16384]{1,0:T(8,128)(2,1)S(1)}, bf16[32,16384]{1,0:T(8,128)(2,1)}, u32[]{:S(2)}) copy-start(bf16[32,16384]{1,0:T(8,128)(2,1)} %param.11) | copy-start | bytes 3145732
  6.5 144.3 %all-gather.2.cloned.1.call-start = ((), (), s32[]{:S(2)}) async-start(), calls=%async_computation.2 | async-start | bytes 6684672 | tf_op jit(solution)/shard_map/all_gather | solution.py:78
  9.0 7.9 %collective-permute-start = (bf16[34,1024]{1,0:T(8,128)(2,1)S(1)}, bf16[34,1024]{1,0:T(8,128)(2,1)S(1)}, u32[]{:S(2)}, u32[]{:S(2)}) collective-permute-start(bf16[34,1024]{1,0:T(8,128)(2,1)S(1)} %get-tuple-element.7), channel_id=1, source_target_pairs={{0,16},{16,32},{32,48},{48,64},{64,80},{80,96},{96,112},{112,128},... | collective-permute-start | bytes 208904 | tf_op jit(solution)/shard_map/ppermute | solution.py:16
  10.9 7.8 %collective-permute-start.1 = (bf16[34,1024]{1,0:T(8,128)(2,1)S(1)}, bf16[34,1024]{1,0:T(8,128)(2,1)S(1)}, u32[]{:S(2)}, u32[]{:S(2)}) collective-permute-start(bf16[34,1024]{1,0:T(8,128)(2,1)S(1)} %get-tuple-element.8), channel_id=1, source_target_pairs={{16,0},{32,16},{48,32},{64,48},{80,64},{96,80},{112,96},{128,112},... | collective-permute-start | bytes 208904 | tf_op jit(solution)/shard_map/ppermute | solution.py:19
  20.5 17.1 %copy-start = (bf16[32,4096]{1,0:T(8,128)(2,1)S(1)}, bf16[32,4096]{1,0:T(8,128)(2,1)}, u32[]{:S(2)}) copy-start(bf16[32,4096]{1,0:T(8,128)(2,1)} %param.6) | copy-start | bytes 786436
  21.6 74.3 %all-to-all-start = ((bf16[32,16,1024]{2,0,1:T(8,128)(2,1)}), bf16[32,16,1024]{2,0,1:T(8,128)(2,1)S(1)}, u32[]{:S(2)}, u32[]{:S(2)}) async-start(bf16[32,16,1024]{2,0,1:T(8,128)(2,1)} %bitcast.59), calls=%async_computation | async-start | bytes 2097152 | tf_op jit(solution)/shard_map/all_to_all | solution.py:85
  36.8 5.5 %copy-start.2 = (f32[1,1024]{1,0:T(1,128)S(1)}, f32[1,1024]{1,0:T(1,128)}, u32[]{:S(2)}) copy-start(f32[1,1024]{1,0:T(1,128)} %param.10) | copy-start | bytes 12292
Sparse Core Ops, SparseCore 0:
  20.6 130.1 all-gather.1
where the time goes:
time: 250 us; the launch traced here: 249 us
  waiting for transfers between devices  110 us (44%)
  blocking collectives  59.4 us (24%)
  local copies, waits for them, and re-layouts  28.2 us (11%)
  starting transfers between devices  22.9 us (9%)
  between operations  14.4 us (6%)
  matrix products  8.31 us (3%)
  other arithmetic  6.37 us (3%)
    all_to_all x1, blocking collectives, on_device(): lax.all_to_all(updated[:, None, :], 'member', split_axis=0, concat_axis=1...  59.4 us
    all_gather x1, waiting for transfers between devices, on_device(): all_rows = lax.all_gather(obs_pool[:ens_dev], 'member', axis=0, tiled=True)  54.4 us
    all_to_all x1, waiting for transfers between devices, on_device(): lax.all_to_all(state_split, 'member', split_axis=1, concat_axis=0, tiled=...  53 us
    all_to_all x1, starting transfers between devices, on_device(): lax.all_to_all(state_split, 'member', split_axis=1, concat_axis=0, tiled=...  15.2 us
    all_gather x1, local copies, waits for them, and re-layouts, on_device(): all_rows = lax.all_gather(obs_pool[:ens_dev], 'member', axis=0, tiled=True)  8.64 us
    gather x1, local copies, waits for them, and re-layouts, on_device(): obs_block = jnp.take(all_rows, own_index, axis=1)  7.58 us
    dot_general x10, matrix products, product_f32(): lax.dot_general(left.astype(jnp.float32), right.astype(jnp.float32), (dim...  5.82 us
    ppermute x1, starting transfers between devices, with_halo(): lax.ppermute(lax.slice_in_dim(block, 0, width, axis=dim), axis, backward)  5.75 us
  transfers between devices with their start and end apart: 4, of which 4 were waited for; matrix products, arithmetic and copies ran while one was open for 3% of the time, Pallas kernels for 0%

commit v1 on v0

v1 whole, which is shorter than its diff:
```python
import functools

import jax
import jax.numpy as jnp
from jax import lax
from jax.experimental import pallas as pl
from jax.experimental.pallas import tpu as pltpu
from jax.sharding import PartitionSpec as P

MESH = pl.DeviceIdType.MESH
F32, BF16 = jnp.float32, jnp.bfloat16
LOC = 1024
NS_ITERS = 3
LANES = 128
ROWS = 128
CHUNKS = 2


def mm(left, right, dims=((1,), (0,)), precision=None):
    return lax.dot_general(
        left, right, (dims, ((), ())), precision=precision, preferred_element_type=F32
    )


def kernel(
    n, tiles,
    hx_ref, pair_ref, index_ref, weight_ref, state_ref,
    out_ref,
    pool, pair_pool, halo, pair_halo, stage, obs, recv, scaled, system, upper, lower, half,
    trans, pert, result,
    halo_send, halo_recv, obs_send, obs_recv, in_send, in_recv, back_send, back_recv, own_sem,
):
    me = lax.axis_index("member")
    tile = lax.axis_index("tile")
    nxt, prv = lax.rem(tile + 1, tiles), lax.rem(tile + tiles - 1, tiles)
    rows = hx_ref.shape[0]
    own = hx_ref.shape[1]
    members = rows * n
    width = LOC // CHUNKS

    def peer(d):
        return lax.rem(me + d, n)

    def nth(k):
        step = n // 2 - (k + 1) // 2
        return jnp.where(k % 2 == 1, step, n - step)

    barrier = pltpu.get_barrier_semaphore()
    for d in range(1, n):
        pl.semaphore_signal(barrier, inc=1, device_id={"member": peer(d)}, device_id_type=MESH)
    for other in (nxt, prv):
        pl.semaphore_signal(barrier, inc=1, device_id={"tile": other}, device_id_type=MESH)

    pool[:, pl.ds(LOC, own)] = hx_ref[...].astype(F32)
    pair_pool[0:2, pl.ds(LOC, own)] = pair_ref[...]

    pl.semaphore_wait(barrier, n + 1)

    def halo_copies():
        copies = []
        for slot, (other, start) in enumerate(((nxt, own - LOC), (prv, 0))):
            for src, dst, place in (
                (hx_ref.at[:, pl.ds(start, LOC)], halo.at[slot], slot),
                (pair_ref.at[:, pl.ds(start, LOC)], pair_halo.at[slot], 2 + slot),
            ):
                copies.append(pltpu.make_async_remote_copy(
                    src_ref=src, dst_ref=dst, send_sem=halo_send.at[place],
                    recv_sem=halo_recv.at[place], device_id={"tile": other}, device_id_type=MESH,
                ))
        return copies

    def in_copy(d, c):
        t = peer(d)
        return pltpu.make_async_remote_copy(
            src_ref=state_ref.at[:, pl.ds(pl.multiple_of(t * LOC + c * width, LANES), width)],
            dst_ref=recv.at[pl.ds(pl.multiple_of(me * rows, rows), rows), pl.ds(c * width, width)],
            send_sem=in_send.at[c, d], recv_sem=in_recv.at[c, d],
            device_id={"member": t}, device_id_type=MESH,
        )

    def obs_copy(d):
        return pltpu.make_async_remote_copy(
            src_ref=stage.at[d],
            dst_ref=obs.at[pl.ds(pl.multiple_of(me * rows, rows), rows), :],
            send_sem=obs_send.at[d], recv_sem=obs_recv.at[d],
            device_id={"member": peer(d)}, device_id_type=MESH,
        )

    def back_copy(d, c):
        t = peer(d)
        return pltpu.make_async_remote_copy(
            src_ref=result.at[pl.ds(pl.multiple_of(t * rows, rows), rows), pl.ds(c * width, width)],
            dst_ref=out_ref.at[:, pl.ds(pl.multiple_of(me * LOC + c * width, LANES), width)],
            send_sem=back_send.at[c, d], recv_sem=back_recv.at[c, d],
            device_id={"member": t}, device_id_type=MESH,
        )

    halos = halo_copies()
    for copy in halos:
        copy.start()

    def start_in(c):
        def body(k, carry):
            in_copy(nth(k), c).start()
            return carry
        lax.fori_loop(0, n - 1, body, 0)

    start_in(0)
    own_state = pltpu.make_async_copy(
        state_ref.at[:, pl.ds(pl.multiple_of(me * LOC, LOC), LOC)],
        recv.at[pl.ds(pl.multiple_of(me * rows, rows), rows), :], own_sem.at[0],
    )
    own_state.start()

    for copy in halos:
        copy.wait()
    for slot, place in ((0, 0), (1, LOC + own)):
        pool[:, pl.ds(place, LOC)] = halo[slot].astype(F32)
        pair_pool[0:2, pl.ds(place, LOC)] = pair_halo[slot]

    def gather(source, height, patch, put):
        row = index_ref[pl.ds(patch, 1), :]
        group, lane = row >> 7, row & (LANES - 1)
        for g in range(LOC // LANES):
            cut = slice(g * LANES, (g + 1) * LANES)
            lane_b = jnp.broadcast_to(lane[:, cut], (height, LANES))
            group_b = jnp.broadcast_to(group[:, cut], (height, LANES))
            value = jnp.zeros((height, LANES), F32)
            for h in range(source.shape[1] // LANES):
                found = jnp.take_along_axis(
                    source[:, h * LANES:(h + 1) * LANES], lane_b, axis=1)
                value = jnp.where(group_b == h, found, value)
            put(cut, value)

    def gather_for(k, carry):
        d = nth(k)

        def put(cut, value):
            stage[d, :, cut] = value.astype(BF16)

        gather(pool, rows, peer(d), put)
        obs_copy(d).start()
        return carry

    lax.fori_loop(0, n - 1, gather_for, 0)
    for c in range(1, CHUNKS):
        start_in(c)

    def put_own(cut, value):
        obs[pl.ds(pl.multiple_of(me * rows, rows), rows), cut] = value.astype(BF16)

    gather(pool, rows, me, put_own)
    sel = []
    gather(pair_pool, pair_pool.shape[0], me, lambda cut, value: sel.append(value))
    value_row = jnp.concatenate([part[0:1] for part in sel], axis=1)
    rinv_row = jnp.concatenate([part[1:2] for part in sel], axis=1)
    root = jnp.sqrt(rinv_row * weight_ref[...])

    def wait_obs(d, carry):
        obs_copy(d).wait()
        return carry

    lax.fori_loop(1, n, wait_obs, 0)

    parts = []
    step = 256
    for s in range(0, LOC, step):
        cut = slice(s, s + step)
        block = obs[:, cut].astype(F32)
        mean = jnp.sum(block, axis=0, keepdims=True) * (1.0 / members)
        scaled[:, cut] = ((block - mean) * root[:, cut]).astype(BF16)
        parts.append((value_row[:, cut] - mean) * root[:, cut])
    innovation = jnp.concatenate(parts, axis=1)
    high = innovation.astype(BF16).astype(F32)
    mid = (innovation - high).astype(BF16).astype(F32)
    low = innovation - high - mid
    split = jnp.concatenate([high, mid, low, jnp.zeros((13, LOC), F32)], axis=0).astype(BF16)
    projection = jnp.sum(mm(split, scaled[...], ((1,), (1,))), axis=0, keepdims=True)

    def eye(r):
        shape = (ROWS, members)
        return (lax.broadcasted_iota(jnp.int32, shape, 0) + r
                == lax.broadcasted_iota(jnp.int32, shape, 1))

    pieces = range(0, members, ROWS)
    square = jnp.zeros((1, members), F32)
    for r in pieces:
        gram = mm(scaled[r:r + ROWS, :], scaled[...], ((1,), (1,)))
        piece = jnp.where(eye(r), gram + (members - 1.0), gram)
        system[r:r + ROWS, :] = piece
        square = square + jnp.sum(piece * piece, axis=0, keepdims=True)
    norm = jnp.sqrt(jnp.sum(square, axis=1, keepdims=True))

    def half_of(product, r):
        scaled_product = -0.5 * product
        return jnp.where(eye(r), 1.5 + scaled_product, scaled_product).astype(BF16)

    for r in pieces:
        first = (system[r:r + ROWS, :] / norm).astype(BF16)
        upper[0, r:r + ROWS, :] = first
        lower[0, r:r + ROWS, :] = half_of(first.astype(F32), r)
    for r in pieces:
        upper[1, r:r + ROWS, :] = mm(upper[0, r:r + ROWS, :], lower[0]).astype(BF16)
    for sweep in range(1, NS_ITERS):
        up, new_up = sweep % 2, (sweep + 1) % 2
        low_now, low_new = (sweep - 1) % 2, sweep % 2
        for r in pieces:
            half[r:r + ROWS, :] = half_of(mm(lower[low_now, r:r + ROWS, :], upper[up]), r)
        if sweep + 1 < NS_ITERS:
            for r in pieces:
                upper[new_up, r:r + ROWS, :] = mm(upper[up, r:r + ROWS, :], half[...]).astype(BF16)
            for r in pieces:
                lower[low_new, r:r + ROWS, :] = mm(half[r:r + ROWS, :], lower[low_now]).astype(BF16)
        else:
            for r in pieces:
                system[r:r + ROWS, :] = mm(half[r:r + ROWS, :], lower[low_now]) / jnp.sqrt(norm)
    invroot = system
    highest = lax.Precision.HIGHEST
    vector = jnp.broadcast_to(projection, (8, members))
    for _ in range(2):
        vector = mm(vector, invroot[...], ((1,), (1,)), highest)
    mean_w = vector[0:1]
    scale = (members - 1.0) ** 0.5
    for r in pieces:
        trans[r:r + ROWS, :] = (scale * invroot[:, r:r + ROWS].T + mean_w).astype(BF16)

    own_state.wait()
    own_back = []
    for c in range(CHUNKS):
        def wait_in(d, carry):
            in_copy(d, c).wait()
            return carry

        lax.fori_loop(1, n, wait_in, 0)
        cut = slice(c * width, (c + 1) * width)
        block = recv[:, cut].astype(F32)
        mean = jnp.sum(block, axis=0, keepdims=True) * (1.0 / members)
        pert[...] = (block - mean).astype(BF16)
        for r in pieces:
            result[r:r + ROWS, cut] = (mean + mm(trans[r:r + ROWS, :], pert[...])).astype(BF16)

        def start_back(k, carry):
            back_copy(nth(k), c).start()
            return carry

        lax.fori_loop(0, n - 1, start_back, 0)
        copy = pltpu.make_async_copy(
            result.at[pl.ds(pl.multiple_of(me * rows, rows), rows), pl.ds(c * width, width)],
            out_ref.at[:, pl.ds(pl.multiple_of(me * LOC + c * width, LANES), width)],
            own_sem.at[1 + c],
        )
        copy.start()
        own_back.append(copy)
    for c in range(CHUNKS):
        def wait_back(d, carry):
            back_copy(d, c).wait()
            return carry

        lax.fori_loop(1, n, wait_back, 0)
        own_back[c].wait()


def on_device(n, tiles, hx, obs_value, obs_rinv, obs_index, loc_weight, state):
    rows, own = hx.shape
    members = rows * n
    pair = jnp.stack([obs_value, obs_rinv]).astype(F32)
    vmem, anywhere = pl.BlockSpec(memory_space=pltpu.VMEM), pl.BlockSpec(memory_space=pl.ANY)
    dma = pltpu.SemaphoreType.DMA
    pool_width = own + 2 * LOC
    return pl.pallas_call(
        functools.partial(kernel, n, tiles),
        out_shape=jax.ShapeDtypeStruct(state.shape, BF16),
        in_specs=[vmem, vmem, vmem, vmem, anywhere],
        out_specs=anywhere,
        scratch_shapes=[
            pltpu.VMEM((rows, pool_width), F32),
            pltpu.VMEM((8, pool_width), F32),
            pltpu.VMEM((2, rows, LOC), BF16),
            pltpu.VMEM((2, 2, LOC), F32),
            pltpu.VMEM((n, rows, LOC), BF16),
            pltpu.VMEM((members, LOC), BF16),
            pltpu.VMEM((members, LOC), BF16),
            pltpu.VMEM((members, LOC), BF16),
            pltpu.VMEM((members, members), F32),
            pltpu.VMEM((2, members, members), BF16),
            pltpu.VMEM((2, members, members), BF16),
            pltpu.VMEM((members, members), BF16),
            pltpu.VMEM((members, members), BF16),
            pltpu.VMEM((members, LOC // CHUNKS), BF16),
            pltpu.VMEM((members, LOC), BF16),
            dma((4,)), dma((4,)), dma((n,)), dma((n,)),
            dma((CHUNKS, n)), dma((CHUNKS, n)), dma((CHUNKS, n)), dma((CHUNKS, n)),
            dma((1 + CHUNKS,)),
        ],
        compiler_params=pltpu.CompilerParams(
            collective_id=0, has_side_effects=True, vmem_limit_bytes=56 << 20
        ),
        cost_estimate=pl.CostEstimate(
            flops=3 * 10**9, bytes_accessed=4 * 2**20, transcendentals=0),
    )(hx, pair, obs_index, loc_weight, state)


def solution(mesh):
    in_specs = (
        P("member", "tile"),
        P("tile"),
        P("tile"),
        P("tile", None),
        P(("tile", "member"), None),
        P("member", "tile"),
    )
    return jax.shard_map(
        functools.partial(on_device, mesh.shape["member"], mesh.shape["tile"]),
        mesh=mesh, in_specs=in_specs, out_specs=P("member", "tile"), check_vma=False,
    )
```

time: 250 us -> 158 us (0.63)
  Pallas kernels: 0 us -> 154 us
  waiting for transfers between devices: 110 us -> 0 us
  blocking collectives: 59.4 us -> 0 us
  local copies, waits for them, and re-layouts: 28.2 us -> 3 us
  starting transfers between devices: 22.9 us -> 0 us
  between operations: 14.4 us -> 0.03 us
  matrix products: 8.31 us -> 0 us
  other arithmetic: 6.37 us -> 0.66 us
    pallas_call x0 -> x1, Pallas kernels: none -> 154 us  [on_device(): pl.pallas_call(functools.partial(kernel, n, tiles), out_shape=jax.ShapeDt...]
    all_to_all x1 -> x0, blocking collectives: 59.4 us -> none  [on_device(): lax.all_to_all(updated[:, None, :], 'member', split_axis=0, concat_axis=1...]
    all_gather x1 -> x0, waiting for transfers between devices: 54.4 us -> none  [on_device(): all_rows = lax.all_gather(obs_pool[:ens_dev], 'member', axis=0, tiled=True)]
    all_to_all x1 -> x0, waiting for transfers between devices: 53 us -> none  [on_device(): lax.all_to_all(state_split, 'member', split_axis=1, concat_axis=0, tiled=...]
    all_to_all x1 -> x0, starting transfers between devices: 15.2 us -> none  [on_device(): lax.all_to_all(state_split, 'member', split_axis=1, concat_axis=0, tiled=...]
    gather x2 -> x0, local copies, waits for them, and re-layouts: 10.8 us -> none  [the longest x1 7.58 us: on_device(): obs_block = jnp.take(all_rows, own_index, axis=1)]
    all_gather x1 -> x0, local copies, waits for them, and re-layouts: 8.64 us -> none  [on_device(): all_rows = lax.all_gather(obs_pool[:ens_dev], 'member', axis=0, tiled=True)]
    dot_general x13 -> x0, matrix products: 8.31 us -> none  [the longest x10 5.82 us: product_f32(): lax.dot_general(left.astype(jnp.float32), right.astype(jnp.float32), (dim...]
  transfers between devices with their start and end apart: 4 -> 0, of which waited for: 4 -> 0; matrix products, arithmetic and copies ran while one was open for 3% -> 0% of each run, Pallas kernels for 0% -> 0%
where the time goes in v1:
time: 158 us; the launch traced here: 157 us
  Pallas kernels  154 us (97%)
  local copies, waits for them, and re-layouts  3 us (2%)
    pallas_call x1, Pallas kernels, on_device(): pl.pallas_call(functools.partial(kernel, n, tiles), out_shape=jax.ShapeDt...  154 us

profile of v1, /device:TPU:24, one launch (start us, length us, event | category | flops | bytes accessed | tf_op | source)
XLA Modules:
  0.0 157.5 jit_solution(16039066118649596145)
XLA Ops:
  0.0 0.0 copy-start
  0.0 0.7 stack.9
  0.7 0.0 copy-done
  0.8 0.7 maximum_convert_fusion.pair_ref
  1.4 153.8 %shard_map.64 = bf16[32,16384]{1,0:T(8,128)(2,1)} custom-call(bf16[32,4096]{1,0:T(8,128)(2,1)} %hx_ref.1, f32[2,4096]{1,0:T(2,128)} %maximum_convert_fusion.pair_ref, s32[16,1024]{1,0:T(8,128)} %index_ref.1, f32[1,1024]{1,0:T(1,128)} %weight_ref.1, bf16[32,16384]{1,0:T(8,128)(2,1)} %state_ref.1), custom_call_target="tpu_custom_call" | custom-call | flops 3000000000 | bytes 4194304 | tf_op jit(solution)/shard_map/pallas_call | solution.py:270
  155.2 2.3 %copy.8 = bf16[32,16384]{1,0:T(8,128)(2,1)} copy(bf16[32,16384]{1,0:T(8,128)(2,1)} %shard_map.64) | data formatting | bytes 2097152
  (1 shorter events, 0.0 us)
Async XLA Ops:
  0.0 0.7 copy-start

commit v2 on v1

v2 whole, which is shorter than its diff:
```python
import functools

import jax
import jax.numpy as jnp
from jax import lax
from jax.experimental import pallas as pl
from jax.experimental.pallas import tpu as pltpu
from jax.sharding import PartitionSpec as P

MESH = pl.DeviceIdType.MESH
F32, BF16 = jnp.float32, jnp.bfloat16
LOC = 1024
NS_ITERS = 3
LANES = 128
ROWS = 128
WINDOW = 17
CHUNKS = 2
FILL = (
    ((0, 4), (0, 3)),
    ((0, 6),),
    ((0, 5),),
    ((0, 7),),
    ((0, 8), (0, 2), (0, 1), (1, 7), (1, 6)),
    ((1, 8), (1, 5), (1, 4), (1, 3), (1, 2), (1, 1)),
)
NEAR = 4
CUTS = 2


def mm(left, right, dims=((1,), (0,)), precision=None):
    return lax.dot_general(
        left, right, (dims, ((), ())), precision=precision, preferred_element_type=F32
    )


def kernel(
    n, tiles,
    hx_ref, pair_ref, index_hbm, weight_hbm, state_ref,
    out_ref,
    pool, wide, pair_pool, pair_wide, index_ref, weight_ref, picked, stage, obs, recv, scaled, system,
    upper, lower, half, trans, pert, result,
    hop_send, hop_recv, halo_send, halo_recv, pair_send, pair_recv, far_send, far_recv,
    in_send, in_recv, back_send, back_recv, own_sem, reach_sem,
):
    me = lax.axis_index("member")
    tile = lax.axis_index("tile")
    nxt, prv = lax.rem(tile + 1, tiles), lax.rem(tile + tiles - 1, tiles)
    rows, own = hx_ref.shape
    members = rows * n
    total = own + 2 * LOC
    width = LOC // CHUNKS
    cut_width = own // CUTS

    def peer(d):
        return lax.rem(me + d + n, n)

    def member_rows(m):
        return pl.ds(pl.multiple_of(m * rows, rows), rows)

    def nth(k):
        step = n // 2 - (k + 1) // 2
        return jnp.where(k % 2 == 1, step, n - step)

    def greet(semaphore, axis, others):
        for other in others:
            pl.semaphore_signal(semaphore, inc=1, device_id={axis: other}, device_id_type=MESH)

    barrier = pltpu.get_barrier_semaphore()
    greet(barrier, "member", (peer(1), peer(-1)))
    greet(barrier, "tile", (nxt, prv))
    local = [
        pltpu.make_async_copy(index_hbm, index_ref, own_sem.at[0]),
        pltpu.make_async_copy(weight_hbm, weight_ref, own_sem.at[1]),
        pltpu.make_async_copy(hx_ref, pool.at[0, :, pl.ds(LOC, own)], own_sem.at[2]),
        pltpu.make_async_copy(
            state_ref.at[:, pl.ds(pl.multiple_of(me * LOC, LOC), LOC)],
            recv.at[member_rows(me), :], own_sem.at[3]),
        pltpu.make_async_copy(pair_ref, pair_pool.at[:, pl.ds(LOC, own)], own_sem.at[4]),
    ]
    for copy in local:
        copy.start()
    pl.semaphore_wait(barrier, 4)

    def hop_copy(h, way, c):
        source = hx_ref if h == 1 else pool.at[2 * h - 3 + way]
        start = c * cut_width
        return pltpu.make_async_remote_copy(
            src_ref=source.at[:, pl.ds(start + (0 if h == 1 else LOC), cut_width)],
            dst_ref=pool.at[2 * h - 1 + way, :, pl.ds(LOC + start, cut_width)],
            send_sem=hop_send.at[h - 1, way, c], recv_sem=hop_recv.at[h - 1, way, c],
            device_id={"member": peer(1 - 2 * way)}, device_id_type=MESH,
        )

    def halo_copy(slot, side):
        source = hx_ref if slot == 0 else pool.at[slot]
        start = (0 if slot == 0 else LOC) + (0 if side else own - LOC)
        return pltpu.make_async_remote_copy(
            src_ref=source.at[:, pl.ds(start, LOC)],
            dst_ref=pool.at[slot, :, pl.ds(LOC + own if side else 0, LOC)],
            send_sem=halo_send.at[slot, side], recv_sem=halo_recv.at[slot, side],
            device_id={"tile": prv if side else nxt}, device_id_type=MESH,
        )

    def pair_copy(side):
        return pltpu.make_async_remote_copy(
            src_ref=pair_ref.at[:, pl.ds(0 if side else own - LOC, LOC)],
            dst_ref=pair_pool.at[:, pl.ds(LOC + own if side else 0, LOC)],
            send_sem=pair_send.at[side], recv_sem=pair_recv.at[side],
            device_id={"tile": prv if side else nxt}, device_id_type=MESH,
        )

    def far_copy(way, j):
        target = peer(j if way == 0 else -j)
        source_rows = member_rows(peer(-NEAR if way == 0 else NEAR))
        lanes = pl.ds(0, LOC)
        if j == n // 2 - NEAR:
            lanes = pl.ds(way * (LOC // 2), LOC // 2)
        return pltpu.make_async_remote_copy(
            src_ref=stage.at[way, j - 1, :, lanes],
            dst_ref=obs.at[source_rows, lanes],
            send_sem=far_send.at[way, j - 1], recv_sem=far_recv.at[way, j - 1],
            device_id={"member": target}, device_id_type=MESH,
        )

    def in_copy(d, c):
        t = peer(d)
        return pltpu.make_async_remote_copy(
            src_ref=state_ref.at[:, pl.ds(pl.multiple_of(t * LOC + c * width, LANES), width)],
            dst_ref=recv.at[member_rows(me), pl.ds(c * width, width)],
            send_sem=in_send.at[c, d], recv_sem=in_recv.at[c, d],
            device_id={"member": t}, device_id_type=MESH,
        )

    def back_copy(d, c):
        t = peer(d)
        return pltpu.make_async_remote_copy(
            src_ref=result.at[member_rows(t), pl.ds(c * width, width)],
            dst_ref=out_ref.at[:, pl.ds(pl.multiple_of(me * LOC + c * width, LANES), width)],
            send_sem=back_send.at[c, d], recv_sem=back_recv.at[c, d],
            device_id={"member": t}, device_id_type=MESH,
        )

    def fill(place):
        for c, d in FILL[place]:
            for distance in sorted({d, n - d}):
                in_copy(distance, c).start()

    for c in range(CUTS):
        for way in range(2):
            hop_copy(1, way, c).start()
    for side in range(2):
        pair_copy(side).start()
        halo_copy(0, side).start()

    known, stage_no = 1, 0
    while known < n // 2:
        greet(reach_sem.at[stage_no], "member", (peer(known), peer(-known)))
        pl.semaphore_wait(reach_sem.at[stage_no], 2)
        known, stage_no = (2 * known if stage_no else 2), stage_no + 1

    for copy in local:
        copy.wait()

    def pick(source, height, patch, puts):
        row = index_ref[pl.ds(patch, 1), :]
        last = total // LANES - WINDOW
        first = jnp.minimum(jnp.min(row, axis=1, keepdims=True) >> 7, last)
        offset = row - first * LANES
        group, lane = offset >> 7, offset & (LANES - 1)
        shape = (8, LANES)
        steps = [bit for bit in (32, 16, 8, 4, 2, 1) if bit <= last]
        chosen = [jnp.broadcast_to(first & bit, shape) != 0 for bit in steps]

        def body(r, carry):
            line = pl.ds(pl.multiple_of(r * 8, 8), 8)
            found = [source[line, h * LANES:(h + 1) * LANES] for h in range(total // LANES)]
            for bit, mask in zip(steps, chosen):
                found = [jnp.where(mask, found[i + bit], found[i])
                         for i in range(min(WINDOW + bit - 1, len(found) - bit))]
            for g in range(LOC // LANES):
                cut = slice(g * LANES, (g + 1) * LANES)
                lane_b = jnp.broadcast_to(lane[:, cut], shape)
                group_b = jnp.broadcast_to(group[:, cut], shape)
                value = jnp.take_along_axis(found[0], lane_b, axis=1)
                for h in range(1, WINDOW):
                    moved = jnp.take_along_axis(found[h], lane_b, axis=1)
                    value = jnp.where(group_b == h, moved, value)
                puts[line, cut] = value
            return carry

        lax.fori_loop(0, height // 8, body, 0)

    def widen(slot):
        wide[...] = pool[slot].astype(F32)

    def near_pick(slot, m):
        for side in range(2):
            halo_copy(slot, side).wait_recv()
        widen(slot)
        pick(wide, rows, me, picked)
        obs[member_rows(m), :] = picked[...].astype(BF16)

    fill(0)
    for h in range(1, NEAR + 1):
        for c in range(CUTS):
            for way in range(2):
                hop_copy(h, way, c).wait_recv()
                if h < NEAR:
                    hop_copy(h + 1, way, c).start()
        for way in range(2):
            for side in range(2):
                halo_copy(2 * h - 1 + way, side).start()
        fill(h)
        if h == 1:
            near_pick(0, me)
        if h > 1:
            for way in range(2):
                near_pick(2 * h - 3 + way, peer((h - 1) * (2 * way - 1)))
    for way in range(2):
        slot = 2 * NEAR - 1 + way
        for side in range(2):
            halo_copy(slot, side).wait_recv()
        widen(slot)
        for j in range(n // 2 - NEAR, 0, -1):
            pick(wide, rows, peer(j if way == 0 else -j), picked)
            stage[way, j - 1] = picked[...].astype(BF16)
            far_copy(way, j).start()
    fill(NEAR + 1)
    for way in range(2):
        widen(2 * NEAR - 1 + way)
        pick(wide, rows, me, picked)
        obs[member_rows(peer(NEAR * (2 * way - 1))), :] = picked[...].astype(BF16)

    for side in range(2):
        pair_copy(side).wait_recv()
    pair_wide[...] = jnp.zeros_like(pair_wide)
    pair_wide[0:2, :] = pair_pool[...]
    pick(pair_wide, 8, me, picked)
    value_row, rinv_row = picked[0:1, :], picked[1:2, :]
    root = jnp.sqrt(rinv_row * weight_ref[...])

    for way in range(2):
        for j in range(n // 2 - NEAR, 0, -1):
            far_copy(way, j).wait()

    parts = []
    step = 256
    for s in range(0, LOC, step):
        cut = slice(s, s + step)
        block = obs[:, cut].astype(F32)
        mean = jnp.sum(block, axis=0, keepdims=True) * (1.0 / members)
        scaled[:, cut] = ((block - mean) * root[:, cut]).astype(BF16)
        parts.append((value_row[:, cut] - mean) * root[:, cut])
    innovation = jnp.concatenate(parts, axis=1)
    high = innovation.astype(BF16).astype(F32)
    mid = (innovation - high).astype(BF16).astype(F32)
    low = innovation - high - mid
    split = jnp.concatenate([high, mid, low, jnp.zeros((13, LOC), F32)], axis=0).astype(BF16)
    projection = jnp.sum(mm(split, scaled[...], ((1,), (1,))), axis=0, keepdims=True)

    def eye(r):
        shape = (ROWS, members)
        return (lax.broadcasted_iota(jnp.int32, shape, 0) + r
                == lax.broadcasted_iota(jnp.int32, shape, 1))

    pieces = range(0, members, ROWS)
    square = jnp.zeros((1, members), F32)
    for r in pieces:
        gram = mm(scaled[r:r + ROWS, :], scaled[...], ((1,), (1,)))
        piece = jnp.where(eye(r), gram + (members - 1.0), gram)
        system[r:r + ROWS, :] = piece
        square = square + jnp.sum(piece * piece, axis=0, keepdims=True)
    norm = jnp.sqrt(jnp.sum(square, axis=1, keepdims=True))

    def half_of(product, r):
        scaled_product = -0.5 * product
        return jnp.where(eye(r), 1.5 + scaled_product, scaled_product).astype(BF16)

    for r in pieces:
        first = (system[r:r + ROWS, :] / norm).astype(BF16)
        upper[0, r:r + ROWS, :] = first
        lower[0, r:r + ROWS, :] = half_of(first.astype(F32), r)
    for r in pieces:
        upper[1, r:r + ROWS, :] = mm(upper[0, r:r + ROWS, :], lower[0]).astype(BF16)
    for sweep in range(1, NS_ITERS):
        up, new_up = sweep % 2, (sweep + 1) % 2
        low_now, low_new = (sweep - 1) % 2, sweep % 2
        for r in pieces:
            half[r:r + ROWS, :] = half_of(mm(lower[low_now, r:r + ROWS, :], upper[up]), r)
        if sweep + 1 < NS_ITERS:
            for r in pieces:
                upper[new_up, r:r + ROWS, :] = mm(upper[up, r:r + ROWS, :], half[...]).astype(BF16)
            for r in pieces:
                lower[low_new, r:r + ROWS, :] = mm(half[r:r + ROWS, :], lower[low_now]).astype(BF16)
        else:
            for r in pieces:
                system[r:r + ROWS, :] = mm(half[r:r + ROWS, :], lower[low_now]) / jnp.sqrt(norm)
    invroot = system
    highest = lax.Precision.HIGHEST
    vector = jnp.broadcast_to(projection, (8, members))
    for _ in range(2):
        vector = mm(vector, invroot[...], ((1,), (1,)), highest)
    mean_w = vector[0:1]
    scale = (members - 1.0) ** 0.5
    for r in pieces:
        trans[r:r + ROWS, :] = (scale * invroot[:, r:r + ROWS].T + mean_w).astype(BF16)

    own_back = []
    for c in range(CHUNKS):
        def wait_in(d, carry):
            in_copy(d, c).wait()
            return carry

        lax.fori_loop(1, n, wait_in, 0)
        cut = slice(c * width, (c + 1) * width)
        block = recv[:, cut].astype(F32)
        mean = jnp.sum(block, axis=0, keepdims=True) * (1.0 / members)
        pert[...] = (block - mean).astype(BF16)
        for r in pieces:
            result[r:r + ROWS, cut] = (mean + mm(trans[r:r + ROWS, :], pert[...])).astype(BF16)

        def start_back(k, carry):
            back_copy(nth(k), c).start()
            return carry

        lax.fori_loop(0, n - 1, start_back, 0)
        copy = pltpu.make_async_copy(
            result.at[member_rows(me), pl.ds(c * width, width)],
            out_ref.at[:, pl.ds(pl.multiple_of(me * LOC + c * width, LANES), width)],
            own_sem.at[5 + c],
        )
        copy.start()
        own_back.append(copy)
    for c in range(CHUNKS):
        def wait_back(d, carry):
            back_copy(d, c).wait()
            return carry

        lax.fori_loop(1, n, wait_back, 0)
        own_back[c].wait()
    for side in range(2):
        pair_copy(side).wait_send()
        for slot in range(2 * NEAR + 1):
            halo_copy(slot, side).wait_send()
    for h in range(1, NEAR + 1):
        for way in range(2):
            for c in range(CUTS):
                hop_copy(h, way, c).wait_send()


def on_device(n, tiles, hx, obs_value, obs_rinv, obs_index, loc_weight, state):
    rows, own = hx.shape
    members = rows * n
    pair = jnp.stack([obs_value, obs_rinv]).astype(F32)
    hbm = pl.BlockSpec(memory_space=pltpu.HBM)
    dma = pltpu.SemaphoreType.DMA
    total = own + 2 * LOC
    return pl.pallas_call(
        functools.partial(kernel, n, tiles),
        out_shape=jax.ShapeDtypeStruct(state.shape, BF16),
        in_specs=[hbm] * 5,
        out_specs=pl.BlockSpec(memory_space=pltpu.VMEM),
        scratch_shapes=[
            pltpu.VMEM((2 * NEAR + 1, rows, total), BF16),
            pltpu.VMEM((rows, total), F32),
            pltpu.VMEM((2, total), F32),
            pltpu.VMEM((8, total), F32),
            pltpu.VMEM((n, LOC), jnp.int32),
            pltpu.VMEM((1, LOC), F32),
            pltpu.VMEM((rows, LOC), F32),
            pltpu.VMEM((2, n // 2 - NEAR, rows, LOC), BF16),
            pltpu.VMEM((members, LOC), BF16),
            pltpu.VMEM((members, LOC), BF16),
            pltpu.VMEM((members, LOC), BF16),
            pltpu.VMEM((members, members), F32),
            pltpu.VMEM((2, members, members), BF16),
            pltpu.VMEM((2, members, members), BF16),
            pltpu.VMEM((members, members), BF16),
            pltpu.VMEM((members, members), BF16),
            pltpu.VMEM((members, LOC // CHUNKS), BF16),
            pltpu.VMEM((members, LOC), BF16),
            dma((NEAR, 2, CUTS)), dma((NEAR, 2, CUTS)),
            dma((2 * NEAR + 1, 2)), dma((2 * NEAR + 1, 2)), dma((2,)), dma((2,)),
            dma((2, n // 2 - NEAR)), dma((2, n // 2 - NEAR)),
            dma((CHUNKS, n)), dma((CHUNKS, n)), dma((CHUNKS, n)), dma((CHUNKS, n)),
            dma((5 + CHUNKS,)), pltpu.SemaphoreType.REGULAR((4,)),
        ],
        compiler_params=pltpu.CompilerParams(
            collective_id=0, has_side_effects=True, vmem_limit_bytes=40 << 20
        ),
        cost_estimate=pl.CostEstimate(
            flops=3 * 10**9, bytes_accessed=4 * 2**20, transcendentals=0),
    )(hx, pair, obs_index, loc_weight, state)


def solution(mesh):
    in_specs = (
        P("member", "tile"),
        P("tile"),
        P("tile"),
        P("tile", None),
        P(("tile", "member"), None),
        P("member", "tile"),
    )
    return jax.shard_map(
        functools.partial(on_device, mesh.shape["member"], mesh.shape["tile"]),
        mesh=mesh, in_specs=in_specs, out_specs=P("member", "tile"), check_vma=False,
    )
```

time: 158 us -> 145 us (0.918)
  Pallas kernels: 154 us -> 139 us
  local copies, waits for them, and re-layouts: 3 us -> 5.22 us
    pallas_call x1, Pallas kernels: 154 us -> 139 us  [on_device(): pl.pallas_call(functools.partial(kernel, n, tiles), out_shape=jax.ShapeDt...]
    unnamed x3 -> x9, local copies, waits for them, and re-layouts: 2.27 us -> 3.77 us
where the time goes in v2:
time: 145 us
  Pallas kernels  139 us (96%)
  local copies, waits for them, and re-layouts  5.22 us (4%)
    pallas_call x1, Pallas kernels, on_device(): pl.pallas_call(functools.partial(kernel, n, tiles), out_shape=jax.ShapeDt...  139 us
    unnamed x9, local copies, waits for them, and re-layouts  3.77 us

profile of v2, /device:TPU:24, one launch (start us, length us, event | category | flops | bytes accessed | tf_op | source)
XLA Modules:
  0.0 144.6 jit_solution(5426168721502267095)
XLA Ops:
  0.0 0.0 copy-start.2
  0.0 0.7 stack.9
  0.7 0.7 stack.10
  1.5 0.0 copy-start.3
  1.5 0.0 copy-done.2
  1.5 0.6 copy-done.3
  2.1 0.0 copy-start
  2.2 1.2 copy-done
  3.4 0.0 copy-start.1
  3.4 0.9 copy-done.1
  4.3 139.3 %shard_map.64 = bf16[32,16384]{1,0:T(8,128)(2,1)S(1)} custom-call(bf16[32,4096]{1,0:T(8,128)(2,1)S(1)} %copy-done.1, f32[2,4096]{1,0:T(2,128)S(1)} %maximum_convert_fusion.pair_ref, s32[16,1024]{1,0:T(8,128)S(1)} %copy-done.2, f32[1,1024]{1,0:T(1,128)S(1)} %copy-done.3, bf16[32,16384]{1,0:T(8,128)(2,1)S(1)} %copy-done), custom_call_target="tpu_custom_call" | custom-call | flops 3000000000 | bytes 4194304 | tf_op jit(solution)/shard_map/pallas_call | solution.py:358
  143.6 1.0 copy.8
  (1 shorter events, 0.0 us)
Async XLA Ops:
  0.0 1.5 %copy-start.2 = (s32[16,1024]{1,0:T(8,128)S(1)}, s32[16,1024]{1,0:T(8,128)}, u32[]{:S(2)}) copy-start(s32[16,1024]{1,0:T(8,128)} %index_hbm.1) | copy-start | bytes 196612
  1.5 0.7 copy-start.3
  2.1 1.2 copy-start
  3.4 0.9 copy-start.1

commit v3 on v2

--- a/solution.py
+++ b/solution.py
@@ -35,9 +35,9 @@
 
 def kernel(
     n, tiles,
-    hx_ref, pair_ref, index_hbm, weight_hbm, state_ref,
+    hx_ref, value_ref, rinv_ref, index_hbm, weight_hbm, state_ref,
     out_ref,
-    pool, wide, pair_pool, pair_wide, index_ref, weight_ref, picked, stage, obs, recv, scaled, system,
+    pool, wide, pairs, pair_wide, index_ref, weight_ref, picked, stage, obs, recv, scaled, system,
     upper, lower, half, trans, pert, result,
     hop_send, hop_recv, halo_send, halo_recv, pair_send, pair_recv, far_send, far_recv,
     in_send, in_recv, back_send, back_recv, own_sem, reach_sem,
@@ -75,7 +75,8 @@
         pltpu.make_async_copy(
             state_ref.at[:, pl.ds(pl.multiple_of(me * LOC, LOC), LOC)],
             recv.at[member_rows(me), :], own_sem.at[3]),
-        pltpu.make_async_copy(pair_ref, pair_pool.at[:, pl.ds(LOC, own)], own_sem.at[4]),
+        pltpu.make_async_copy(value_ref, pairs.at[0, 1], own_sem.at[4]),
+        pltpu.make_async_copy(rinv_ref, pairs.at[1, 1], own_sem.at[5]),
     ]
     for copy in local:
         copy.start()
@@ -101,11 +102,11 @@
             device_id={"tile": prv if side else nxt}, device_id_type=MESH,
         )
 
-    def pair_copy(side):
-        return pltpu.make_async_remote_copy(
-            src_ref=pair_ref.at[:, pl.ds(0 if side else own - LOC, LOC)],
-            dst_ref=pair_pool.at[:, pl.ds(LOC + own if side else 0, LOC)],
-            send_sem=pair_send.at[side], recv_sem=pair_recv.at[side],
+    def pair_copy(which, side):
+        return pltpu.make_async_remote_copy(
+            src_ref=rinv_ref if which else value_ref,
+            dst_ref=pairs.at[which, 2 if side else 0],
+            send_sem=pair_send.at[which, side], recv_sem=pair_recv.at[which, side],
             device_id={"tile": prv if side else nxt}, device_id_type=MESH,
         )
 
@@ -149,7 +150,8 @@
         for way in range(2):
             hop_copy(1, way, c).start()
     for side in range(2):
-        pair_copy(side).start()
+        for which in range(2):
+            pair_copy(which, side).start()
         halo_copy(0, side).start()
 
     known, stage_no = 1, 0
@@ -231,10 +233,15 @@
         pick(wide, rows, me, picked)
         obs[member_rows(peer(NEAR * (2 * way - 1))), :] = picked[...].astype(BF16)
 
-    for side in range(2):
-        pair_copy(side).wait_recv()
     pair_wide[...] = jnp.zeros_like(pair_wide)
-    pair_wide[0:2, :] = pair_pool[...]
+    for which in range(2):
+        for side in range(2):
+            pair_copy(which, side).wait_recv()
+        lines = [pairs[which, place].astype(F32) for place in range(3)]
+        edge = LOC // LANES
+        lines = jnp.concatenate([lines[0][own // LANES - edge:], lines[1], lines[2][:edge]], axis=0)
+        for h in range(total // LANES):
+            pair_wide[which:which + 1, h * LANES:(h + 1) * LANES] = lines[h:h + 1, :]
     pick(pair_wide, 8, me, picked)
     value_row, rinv_row = picked[0:1, :], picked[1:2, :]
     root = jnp.sqrt(rinv_row * weight_ref[...])
@@ -327,7 +334,7 @@
         copy = pltpu.make_async_copy(
             result.at[member_rows(me), pl.ds(c * width, width)],
             out_ref.at[:, pl.ds(pl.multiple_of(me * LOC + c * width, LANES), width)],
-            own_sem.at[5 + c],
+            own_sem.at[6 + c],
         )
         copy.start()
         own_back.append(copy)
@@ -339,7 +346,8 @@
         lax.fori_loop(1, n, wait_back, 0)
         own_back[c].wait()
     for side in range(2):
-        pair_copy(side).wait_send()
+        for which in range(2):
+            pair_copy(which, side).wait_send()
         for slot in range(2 * NEAR + 1):
             halo_copy(slot, side).wait_send()
     for h in range(1, NEAR + 1):
@@ -351,19 +359,19 @@
 def on_device(n, tiles, hx, obs_value, obs_rinv, obs_index, loc_weight, state):
     rows, own = hx.shape
     members = rows * n
-    pair = jnp.stack([obs_value, obs_rinv]).astype(F32)
+    value, rinv = obs_value.reshape(own // LANES, LANES), obs_rinv.reshape(own // LANES, LANES)
     hbm = pl.BlockSpec(memory_space=pltpu.HBM)
     dma = pltpu.SemaphoreType.DMA
     total = own + 2 * LOC
     return pl.pallas_call(
         functools.partial(kernel, n, tiles),
         out_shape=jax.ShapeDtypeStruct(state.shape, BF16),
-        in_specs=[hbm] * 5,
+        in_specs=[hbm] * 6,
         out_specs=pl.BlockSpec(memory_space=pltpu.VMEM),
         scratch_shapes=[
             pltpu.VMEM((2 * NEAR + 1, rows, total), BF16),
             pltpu.VMEM((rows, total), F32),
-            pltpu.VMEM((2, total), F32),
+            pltpu.VMEM((2, 3, own // LANES, LANES), BF16),
             pltpu.VMEM((8, total), F32),
             pltpu.VMEM((n, LOC), jnp.int32),
             pltpu.VMEM((1, LOC), F32),
@@ -380,17 +388,18 @@
             pltpu.VMEM((members, LOC // CHUNKS), BF16),
             pltpu.VMEM((members, LOC), BF16),
             dma((NEAR, 2, CUTS)), dma((NEAR, 2, CUTS)),
-            dma((2 * NEAR + 1, 2)), dma((2 * NEAR + 1, 2)), dma((2,)), dma((2,)),
+            dma((2 * NEAR + 1, 2)), dma((2 * NEAR + 1, 2)), dma((2, 2)), dma((2, 2)),
             dma((2, n // 2 - NEAR)), dma((2, n // 2 - NEAR)),
             dma((CHUNKS, n)), dma((CHUNKS, n)), dma((CHUNKS, n)), dma((CHUNKS, n)),
-            dma((5 + CHUNKS,)), pltpu.SemaphoreType.REGULAR((4,)),
+            dma((6 + CHUNKS,)), pltpu.SemaphoreType.REGULAR((4,)),
         ],
         compiler_params=pltpu.CompilerParams(
             collective_id=0, has_side_effects=True, vmem_limit_bytes=40 << 20
         ),
         cost_estimate=pl.CostEstimate(
             flops=3 * 10**9, bytes_accessed=4 * 2**20, transcendentals=0),
-    )(hx, pair, obs_index, loc_weight, state)
+    )(*(pltpu.with_memory_space_constraint(x, pltpu.HBM)
+        for x in (hx, value, rinv, obs_index, loc_weight, state)))
 
 
 def solution(mesh):

time: 145 us -> 142 us (0.979)
  local copies, waits for them, and re-layouts: 5.22 us -> 0.97 us
    unnamed x9 -> x1, local copies, waits for them, and re-layouts: 3.77 us -> 0.97 us
where the time goes in v3:
time: 142 us; the launch traced here: 141 us
  Pallas kernels  140 us (99%)
    pallas_call x1, Pallas kernels, on_device(): pl.pallas_call(functools.partial(kernel, n, tiles), out_shape=jax.ShapeDt...  140 us

profile of v3, /device:TPU:24, one launch (start us, length us, event | category | flops | bytes accessed | tf_op | source)
XLA Modules:
  0.0 140.5 jit_solution(4562939773863785379)
XLA Ops:
  0.0 139.5 %shard_map.64 = bf16[32,16384]{1,0:T(8,128)(2,1)S(1)} custom-call(bf16[32,4096]{1,0:T(8,128)(2,1)} %hx_ref.1, bf16[32,128]{1,0:T(8,128)(2,1)} %bitcast.2, bf16[32,128]{1,0:T(8,128)(2,1)} %bitcast.3, s32[16,1024]{1,0:T(8,128)} %index_hbm.1, f32[1,1024]{1,0:T(1,128)} %weight_hbm.1, bf16[32,16384]{1,0:T(8,128)(2,1)} %state_ref.1), custom_call_target="tpu_custom_call" | custom-call | flops 3000000000 | bytes 4194304 | tf_op jit(solution)/shard_map/pallas_call | solution.py:366
  139.5 1.0 copy.8

commit v4 on v3

--- a/solution.py
+++ b/solution.py
@@ -16,12 +16,12 @@
 WINDOW = 17
 CHUNKS = 2
 FILL = (
-    ((0, 4), (0, 3)),
+    ((0, 2), (0, 3)),
+    ((0, 5),),
+    ((0, 4), (0, 1)),
     ((0, 6),),
-    ((0, 5),),
-    ((0, 7),),
-    ((0, 8), (0, 2), (0, 1), (1, 7), (1, 6)),
-    ((1, 8), (1, 5), (1, 4), (1, 3), (1, 2), (1, 1)),
+    ((0, 7), (0, 8), (1, 6), (1, 4)),
+    ((1, 8), (1, 7), (1, 5), (1, 3), (1, 2), (1, 1)),
 )
 NEAR = 4
 CUTS = 2
@@ -192,14 +192,14 @@
 
         lax.fori_loop(0, height // 8, body, 0)
 
-    def widen(slot):
-        wide[...] = pool[slot].astype(F32)
+    def widen(slot, way=0):
+        wide[way] = pool[slot].astype(F32)
 
     def near_pick(slot, m):
         for side in range(2):
             halo_copy(slot, side).wait_recv()
         widen(slot)
-        pick(wide, rows, me, picked)
+        pick(wide.at[0], rows, me, picked)
         obs[member_rows(m), :] = picked[...].astype(BF16)
 
     fill(0)
@@ -222,15 +222,15 @@
         slot = 2 * NEAR - 1 + way
         for side in range(2):
             halo_copy(slot, side).wait_recv()
-        widen(slot)
-        for j in range(n // 2 - NEAR, 0, -1):
-            pick(wide, rows, peer(j if way == 0 else -j), picked)
+        widen(slot, way)
+    for j in range(n // 2 - NEAR, 0, -1):
+        for way in range(2):
+            pick(wide.at[way], rows, peer(j if way == 0 else -j), picked)
             stage[way, j - 1] = picked[...].astype(BF16)
             far_copy(way, j).start()
     fill(NEAR + 1)
     for way in range(2):
-        widen(2 * NEAR - 1 + way)
-        pick(wide, rows, me, picked)
+        pick(wide.at[way], rows, me, picked)
         obs[member_rows(peer(NEAR * (2 * way - 1))), :] = picked[...].astype(BF16)
 
     pair_wide[...] = jnp.zeros_like(pair_wide)
@@ -370,7 +370,7 @@
         out_specs=pl.BlockSpec(memory_space=pltpu.VMEM),
         scratch_shapes=[
             pltpu.VMEM((2 * NEAR + 1, rows, total), BF16),
-            pltpu.VMEM((rows, total), F32),
+            pltpu.VMEM((2, rows, total), F32),
             pltpu.VMEM((2, 3, own // LANES, LANES), BF16),
             pltpu.VMEM((8, total), F32),
             pltpu.VMEM((n, LOC), jnp.int32),

time: 142 us -> 141 us (level)
  no operation moved by 1% of the time
where the time goes in v4:
time: 141 us
  Pallas kernels  140 us (99%)
    pallas_call x1, Pallas kernels, on_device(): pl.pallas_call(functools.partial(kernel, n, tiles), out_shape=jax.ShapeDt...  140 us

profile of v4, /device:TPU:24, one launch (start us, length us, event | category | flops | bytes accessed | tf_op | source)
XLA Modules:
  0.0 140.6 jit_solution(10864070430289766952)
XLA Ops:
  0.0 139.6 %shard_map.64 = bf16[32,16384]{1,0:T(8,128)(2,1)S(1)} custom-call(bf16[32,4096]{1,0:T(8,128)(2,1)} %hx_ref.1, bf16[32,128]{1,0:T(8,128)(2,1)} %bitcast.2, bf16[32,128]{1,0:T(8,128)(2,1)} %bitcast.3, s32[16,1024]{1,0:T(8,128)} %index_hbm.1, f32[1,1024]{1,0:T(1,128)} %weight_hbm.1, bf16[32,16384]{1,0:T(8,128)(2,1)} %state_ref.1), custom_call_target="tpu_custom_call" | custom-call | flops 3000000000 | bytes 4194304 | tf_op jit(solution)/shard_map/pallas_call | solution.py:366
  139.6 1.0 copy.8

commit v5 on v4

--- a/solution.py
+++ b/solution.py
@@ -24,7 +24,7 @@
     ((1, 8), (1, 7), (1, 5), (1, 3), (1, 2), (1, 1)),
 )
 NEAR = 4
-CUTS = 2
+CUTS = 1
 
 
 def mm(left, right, dims=((1,), (0,)), precision=None):

time: 141 us -> 142 us (level)
  no operation moved by 1% of the time
where the time goes in v5:
time: 142 us; the launch traced here: 141 us
  Pallas kernels  140 us (99%)
    pallas_call x1, Pallas kernels, on_device(): pl.pallas_call(functools.partial(kernel, n, tiles), out_shape=jax.ShapeDt...  140 us

profile of v5, /device:TPU:24, one launch (start us, length us, event | category | flops | bytes accessed | tf_op | source)
XLA Modules:
  0.0 140.6 jit_solution(16867228884140527872)
XLA Ops:
  0.0 139.7 %shard_map.64 = bf16[32,16384]{1,0:T(8,128)(2,1)S(1)} custom-call(bf16[32,4096]{1,0:T(8,128)(2,1)} %hx_ref.1, bf16[32,128]{1,0:T(8,128)(2,1)} %bitcast.2, bf16[32,128]{1,0:T(8,128)(2,1)} %bitcast.3, s32[16,1024]{1,0:T(8,128)} %index_hbm.1, f32[1,1024]{1,0:T(1,128)} %weight_hbm.1, bf16[32,16384]{1,0:T(8,128)(2,1)} %state_ref.1), custom_call_target="tpu_custom_call" | custom-call | flops 3000000000 | bytes 4194304 | tf_op jit(solution)/shard_map/pallas_call | solution.py:366
  139.7 1.0 copy.8
